TPU v7x, 512 devices: a whole 4x4x16 slice. The times are simulated.
512 devices in a mesh: head: 8 (over x, core), tok: 64 (over z, y).
Axes of the slice: x: 4, y: 4, z: 16, core: 2. Of those that a mesh axis runs over, the one named last changes fastest.
Arguments:
- query_one: bfloat16 [16384, 4096], P(('head', 'tok')), may hold values from -6 to 6
- key_one: bfloat16 [16384, 4096], P(('head', 'tok')), may hold values from -6 to 6
- value_one: bfloat16 [16384, 4096], P(('head', 'tok')), may hold values from -6 to 6
- rate_one: bfloat16 [16384, 8], P(('head', 'tok')), may hold values from 0.099609375 to 1
- query_two: bfloat16 [16384, 4096], P(('head', 'tok')), may hold values from -6 to 6
- w_gate: float32 [8, 512, 512], P('head', 'tok'), may hold values from -0.25 to 0.25
- w_up: float32 [8, 512, 512], P('head', 'tok'), may hold values from -0.25 to 0.25
- w_down: float32 [8, 512, 512], P('head', 'tok'), may hold values from -0.25 to 0.25
- step_size: float32 [8], P('head'), may hold values from 0.02 to 0.08
Outputs:
- out_one: bfloat16 [16384, 4096], P(('head', 'tok'))
- out_two: bfloat16 [16384, 4096], P(('head', 'tok'))
- gate_new: float32 [8, 512, 512], P('head', 'tok')
- up_new: float32 [8, 512, 512], P('head', 'tok')
- down_new: float32 [8, 512, 512], P('head', 'tok')
All inputs are finite; a program needn't handle non-finite values.
Results may differ from a plain program's by a relative error of at most 0.011.
Values may be sent and summed in bfloat16 or wider, within the bound.
A program may use at most 64 MiB of HBM per device.

v0:
```python
import jax
import jax.numpy as jnp
from jax import lax
from jax.sharding import PartitionSpec as P


def apply_piece(query, gate_b, up_b, down_b):
    pre_gate = jnp.einsum("thd,hjd->htj", query, gate_b, preferred_element_type=jnp.float32)
    pre_up = jnp.einsum("thd,hjd->htj", query, up_b, preferred_element_type=jnp.float32)
    hidden = (pre_gate * jax.nn.sigmoid(pre_gate) * pre_up).astype(jnp.bfloat16)
    return jnp.einsum("htj,hjd->thd", hidden, down_b, preferred_element_type=jnp.float32)


def forward_piece(query, keys, targets, gate_b, up_b, down_b):
    out_term = apply_piece(query, gate_b, up_b, down_b)
    key_gate = jnp.einsum("thd,hjd->htj", keys, gate_b, preferred_element_type=jnp.float32)
    key_up = jnp.einsum("thd,hjd->htj", keys, up_b, preferred_element_type=jnp.float32)
    sigmoid_k = jax.nn.sigmoid(key_gate)
    act_k = key_gate * sigmoid_k
    hidden_k = (act_k * key_up).astype(jnp.bfloat16)
    back = jnp.einsum("thd,hjd->htj", targets, down_b, preferred_element_type=jnp.float32)
    grad_gate_pre = (back * key_up * sigmoid_k * (1.0 + key_gate * (1.0 - sigmoid_k))).astype(
        jnp.bfloat16
    )
    grad_up_pre = (back * act_k).astype(jnp.bfloat16)
    return (out_term, grad_gate_pre, grad_up_pre, hidden_k)


def gradient_rows(gate_all, up_all, hidden_all, keys, targets):
    grad_gate = jnp.einsum("htj,thd->jhd", gate_all, keys, preferred_element_type=jnp.float32)
    grad_up = jnp.einsum("htj,thd->jhd", up_all, keys, preferred_element_type=jnp.float32)
    grad_down = jnp.einsum("htj,thd->jhd", hidden_all, targets, preferred_element_type=jnp.float32)
    return jnp.stack([grad_gate, grad_up, grad_down], axis=2)


def renew(weights, grad_rows, step_size):
    grads = jnp.moveaxis(grad_rows, 0, 1)
    scale = jnp.sqrt(jnp.mean(grads * grads, axis=2, keepdims=True) + 1e-06)
    return weights - step_size[:, None, None] * grads / scale


def local(query_one, key_one, value_one, rate_one, query_two, w_gate, w_up, w_down, step_size):
    heads_local = w_gate.shape[0]
    width = w_gate.shape[2]
    moved = (
        lax.all_to_all(query_one, "head", split_axis=1, concat_axis=0, tiled=True),
        lax.all_to_all(key_one, "head", split_axis=1, concat_axis=0, tiled=True),
        lax.all_to_all(value_one, "head", split_axis=1, concat_axis=0, tiled=True),
        lax.all_to_all(rate_one, "head", split_axis=1, concat_axis=0, tiled=True),
        lax.all_to_all(query_two, "head", split_axis=1, concat_axis=0, tiled=True),
    )
    tokens = moved[0].shape[0]
    query_a = moved[0].reshape(tokens, heads_local, width)
    keys = moved[1].reshape(tokens, heads_local, width)
    values = moved[2].reshape(tokens, heads_local, width)
    rates = moved[3].astype(jnp.float32)
    query_b = moved[4].reshape(tokens, heads_local, width)
    targets = (-(rates[:, :, None] * values.astype(jnp.float32))).astype(jnp.bfloat16)
    pieces = (
        lax.all_gather(w_gate.astype(jnp.bfloat16), "tok", axis=1, tiled=True),
        lax.all_gather(w_up.astype(jnp.bfloat16), "tok", axis=1, tiled=True),
        lax.all_gather(w_down.astype(jnp.bfloat16), "tok", axis=1, tiled=True),
    )
    out_term, grad_gate_pre, grad_up_pre, hidden_k = forward_piece(
        query_a, keys, targets, pieces[0], pieces[1], pieces[2]
    )
    first_block = out_term.reshape(tokens, heads_local * width).astype(jnp.bfloat16)
    grad_local = lax.psum_scatter(
        gradient_rows(grad_gate_pre, grad_up_pre, hidden_k, keys, targets),
        "tok",
        scatter_dimension=0,
        tiled=True,
    )
    gate_new = renew(w_gate, grad_local[:, :, 0, :], step_size)
    up_new = renew(w_up, grad_local[:, :, 1, :], step_size)
    down_new = renew(w_down, grad_local[:, :, 2, :], step_size)
    pieces = (
        lax.all_gather(gate_new.astype(jnp.bfloat16), "tok", axis=1, tiled=True),
        lax.all_gather(up_new.astype(jnp.bfloat16), "tok", axis=1, tiled=True),
        lax.all_gather(down_new.astype(jnp.bfloat16), "tok", axis=1, tiled=True),
    )
    second_total = apply_piece(query_b, pieces[0], pieces[1], pieces[2])
    second_block = second_total.reshape(tokens, heads_local * width).astype(jnp.bfloat16)
    first_back, second_back = (
        lax.all_to_all(first_block, "head", split_axis=0, concat_axis=1, tiled=True),
        lax.all_to_all(second_block, "head", split_axis=0, concat_axis=1, tiled=True),
    )
    return (first_back, second_back, gate_new, up_new, down_new)


def solution(mesh):
    in_specs = (
        P(("head", "tok"), None),
        P(("head", "tok"), None),
        P(("head", "tok"), None),
        P(("head", "tok"), None),
        P(("head", "tok"), None),
        P("head", "tok", None),
        P("head", "tok", None),
        P("head", "tok", None),
        P("head"),
    )
    out_specs = (
        P(("head", "tok"), None),
        P(("head", "tok"), None),
        P("head", "tok", None),
        P("head", "tok", None),
        P("head", "tok", None),
    )
    return jax.shard_map(local, mesh=mesh, in_specs=in_specs, out_specs=out_specs, check_vma=False)
```

profile of v0, /device:TPU:1, one launch (start us, length us, event | category | flops | bytes accessed | tf_op | source)
XLA Modules:
  0.0 1364.1 jit_solution(18135310961557693874)
XLA Ops:
  7.2 1.3 copy.43
  8.4 10.1 all-to-all-start.2
  18.5 0.7 convert_element_type.143
  19.3 76.5 %all_gather.20 = bf16[1,512,512]{2,1,0:T(8,128)(2,1)S(1)} all-gather(bf16[1,8,512]{2,1,0:T(8,128)(2,1)S(1)} %convert_element_type.143), channel_id=1, replica_groups=mesh['head'=8,'tok'=64] {'tok'}, dimensions={1}, use_global_device_ids=true | all-gather | bytes 532480 | tf_op jit(solution)/shard_map/all_gather | solution.py:62
  95.8 0.7 convert_element_type.141
  96.5 73.1 %all_gather.19 = bf16[1,512,512]{2,1,0:T(8,128)(2,1)S(1)} all-gather(bf16[1,8,512]{2,1,0:T(8,128)(2,1)S(1)} %convert_element_type.141), channel_id=1, replica_groups=mesh['head'=8,'tok'=64] {'tok'}, dimensions={1}, use_global_device_ids=true | all-gather | bytes 532480 | tf_op jit(solution)/shard_map/all_gather | solution.py:61
  169.7 0.7 convert_element_type.140
  170.4 1.7 copy.66
  172.0 1.7 copy.65
  173.7 0.0 all-to-all-done.2
  173.7 55.9 %all-to-all-start.4 = ((bf16[32,8,512]{2,0,1:T(8,128)(2,1)}), bf16[32,8,512]{2,0,1:T(8,128)(2,1)S(1)}, u32[]{:S(2)}, u32[]{:S(2)}) async-start(bf16[32,8,512]{2,0,1:T(8,128)(2,1)} %bitcast.139), calls=%async_computation.4 | async-start | bytes 524288 | tf_op jit(solution)/shard_map/all_to_all | solution.py:47
  229.7 71.9 %all_gather.18 = bf16[1,512,512]{2,1,0:T(8,128)(2,1)S(1)} all-gather(bf16[1,8,512]{2,1,0:T(8,128)(2,1)S(1)} %convert_element_type.140), channel_id=1, replica_groups=mesh['head'=8,'tok'=64] {'tok'}, dimensions={1}, use_global_device_ids=true | all-gather | bytes 532480 | tf_op jit(solution)/shard_map/all_gather | solution.py:60
  301.6 0.1 reshape.421
  301.7 0.0 all-to-all-done.4
  301.7 30.4 %all-to-all-start.3 = ((bf16[32,8,512]{2,0,1:T(8,128)(2,1)}), bf16[32,8,512]{2,0,1:T(8,128)(2,1)S(1)}, u32[]{:S(2)}, u32[]{:S(2)}) async-start(bf16[32,8,512]{2,0,1:T(8,128)(2,1)} %bitcast.140), calls=%async_computation.3 | async-start | bytes 524288 | tf_op jit(solution)/shard_map/all_to_all | solution.py:48
  332.0 0.0 reduce-scatter.2.cloned.1.call-start
  332.0 0.3 fusion.12
  332.4 0.3 fusion.16
  332.7 5.8 all-to-all-done.3
  338.6 0.3 fusion.9
  338.9 0.4 convolution_bitcast_fusion.1
  339.3 0.4 convolution_bitcast_fusion.2
  339.8 0.1 fusion.4
  339.9 0.4 convolution_bitcast_fusion
  340.3 1.9 pad_maximum_fusion
  342.2 0.0 copy-start
  342.2 0.0 copy-start.1
  342.2 0.0 reduce-scatter.2.cloned.1.call-update
  342.2 0.9 copy-done
  343.2 0.7 copy.67
  343.9 4.4 all-to-all-start
  348.2 0.0 copy-done.1
  348.3 0.0 copy-start.2
  348.3 0.0 copy-start.3
  348.3 0.0 copy-start.4
  348.3 0.7 copy.64
  349.7 5.1 all-to-all-done
  354.8 4.4 all-to-all-start.5
  359.1 0.3 fusion.18
  359.5 1.3 convolution_convert_fusion.1
  360.7 665.9 %reduce-scatter.2.cloned.1.call-done = f32[8,1,3,512]{3,0,2,1:T(8,128)} async-done(((f32[512,1,3,512]{3,0,2,1:T(8,128)}), f32[8,1,3,512]{3,0,2,1:T(8,128)}) %reduce-scatter.2.cloned.1.call-update) | async-done | bytes 49168 | tf_op jit(solution)/shard_map/reduce_scatter | solution.py:68
  1026.6 0.9 multiply_reduce_fusion.1
  1027.5 0.0 copy-done.2
  1027.5 0.0 copy-done.3
  1027.6 0.0 copy-done.4
  1027.6 1.5 fusion.47
  1029.0 72.6 %all_gather.23 = bf16[1,512,512]{2,1,0:T(8,128)(2,1)S(1)} all-gather(bf16[1,8,512]{2,1,0:T(8,128)(2,1)S(1)} %get-tuple-element.14), channel_id=1, replica_groups=mesh['head'=8,'tok'=64] {'tok'}, dimensions={1}, use_global_device_ids=true | all-gather | bytes 532480 | tf_op jit(solution)/shard_map/all_gather | solution.py:79
  1101.6 73.4 %all_gather.21 = bf16[1,512,512]{2,1,0:T(8,128)(2,1)S(1)} all-gather(bf16[1,8,512]{2,1,0:T(8,128)(2,1)S(1)} %get-tuple-element.16), channel_id=1, replica_groups=mesh['head'=8,'tok'=64] {'tok'}, dimensions={1}, use_global_device_ids=true | all-gather | bytes 532480 | tf_op jit(solution)/shard_map/all_gather | solution.py:80
  1175.0 72.8 %all_gather.22 = bf16[1,512,512]{2,1,0:T(8,128)(2,1)S(1)} all-gather(bf16[1,8,512]{2,1,0:T(8,128)(2,1)S(1)} %get-tuple-element.8), channel_id=1, replica_groups=mesh['head'=8,'tok'=64] {'tok'}, dimensions={1}, use_global_device_ids=true | all-gather | bytes 532480 | tf_op jit(solution)/shard_map/all_gather | solution.py:78
  1247.8 0.0 all-to-all-done.5
  1247.8 91.3 %all-to-all-start.1 = ((bf16[8,32,512]{2,1,0:T(8,128)(2,1)}), bf16[8,32,512]{2,1,0:T(8,128)(2,1)S(1)}, u32[]{:S(2)}, u32[]{:S(2)}) async-start(bf16[8,32,512]{2,1,0:T(8,128)(2,1)} %bitcast.9), calls=%async_computation.1 | async-start | bytes 524288 | tf_op jit(solution)/shard_map/all_to_all | solution.py:85
  1339.1 0.3 convolution_bitcast_fusion.4
  1339.5 1.3 convolution_convert_fusion
  1340.7 4.9 all-to-all-done.1
  1345.6 4.4 all-to-all-start.6
  1350.0 0.7 copy.58
  1350.7 5.8 all-to-all-done.6
  1356.5 0.7 copy.59
  (4 shorter events, 0.1 us)
Async XLA Ops:
  8.4 165.3 %all-to-all-start.2 = ((bf16[32,8,1]{0,2,1:T(2,128)(2,1)}), bf16[32,8,1]{0,2,1:T(2,128)(2,1)S(1)}, u32[]{:S(2)}, u32[]{:S(2)}) async-start(bf16[32,8,1]{0,2,1:T(2,128)(2,1)} %copy.43), calls=%async_computation.2 | async-start | bytes 8192 | tf_op jit(solution)/shard_map/all_to_all | solution.py:49
  173.7 128.0 %all-to-all-start.4 = ((bf16[32,8,512]{2,0,1:T(8,128)(2,1)}), bf16[32,8,512]{2,0,1:T(8,128)(2,1)S(1)}, u32[]{:S(2)}, u32[]{:S(2)}) async-start(bf16[32,8,512]{2,0,1:T(8,128)(2,1)} %bitcast.139), calls=%async_computation.4 | async-start | bytes 524288 | tf_op jit(solution)/shard_map/all_to_all | solution.py:47
  301.7 36.9 %all-to-all-start.3 = ((bf16[32,8,512]{2,0,1:T(8,128)(2,1)}), bf16[32,8,512]{2,0,1:T(8,128)(2,1)S(1)}, u32[]{:S(2)}, u32[]{:S(2)}) async-start(bf16[32,8,512]{2,0,1:T(8,128)(2,1)} %bitcast.140), calls=%async_computation.3 | async-start | bytes 524288 | tf_op jit(solution)/shard_map/all_to_all | solution.py:48
  332.0 694.6 %reduce-scatter.2.cloned.1.call-start = ((), (), s32[]{:S(2)}) async-start(), calls=%async_computation.8 | async-start | bytes 3194880 | tf_op jit(solution)/shard_map/reduce_scatter | solution.py:68
  342.2 0.9 copy-start
  342.2 6.0 copy-start.1
  343.9 10.9 all-to-all-start
  348.3 679.3 %copy-start.2 = (f32[1,8,512]{2,1,0:T(8,128)S(1)}, f32[1,8,512]{2,1,0:T(8,128)}, u32[]{:S(2)}) copy-start(f32[1,8,512]{2,1,0:T(8,128)} %param.16) | copy-start | bytes 49156
  348.3 679.3 %copy-start.3 = (f32[1,8,512]{2,1,0:T(8,128)S(1)}, f32[1,8,512]{2,1,0:T(8,128)}, u32[]{:S(2)}) copy-start(f32[1,8,512]{2,1,0:T(8,128)} %param.15) | copy-start | bytes 49156
  348.3 679.3 %copy-start.4 = (f32[1,8,512]{2,1,0:T(8,128)S(1)}, f32[1,8,512]{2,1,0:T(8,128)}, u32[]{:S(2)}) copy-start(f32[1,8,512]{2,1,0:T(8,128)} %param.14) | copy-start | bytes 49156
  354.8 893.0 %all-to-all-start.5 = ((bf16[32,8,512]{2,0,1:T(8,128)(2,1)}), bf16[32,8,512]{2,0,1:T(8,128)(2,1)S(1)}, u32[]{:S(2)}, u32[]{:S(2)}) async-start(bf16[32,8,512]{2,0,1:T(8,128)(2,1)} %bitcast.138), calls=%async_computation.6 | async-start | bytes 524288 | tf_op jit(solution)/shard_map/all_to_all | solution.py:50
  1247.8 97.8 %all-to-all-start.1 = ((bf16[8,32,512]{2,1,0:T(8,128)(2,1)}), bf16[8,32,512]{2,1,0:T(8,128)(2,1)S(1)}, u32[]{:S(2)}, u32[]{:S(2)}) async-start(bf16[8,32,512]{2,1,0:T(8,128)(2,1)} %bitcast.9), calls=%async_computation.1 | async-start | bytes 524288 | tf_op jit(solution)/shard_map/all_to_all | solution.py:85
  1345.6 10.9 all-to-all-start.6
Sparse Core Ops, SparseCore 0:
  342.4 684.1 reduce-scatter.1
where the time goes:
time: 1370 us; the launch traced here: 1360 us
  waiting for transfers between devices  688 us (50%)
  blocking collectives  440 us (32%)
  starting transfers between devices  201 us (15%)
  between operations  14.8 us (1%)
    reduce_scatter x1, waiting for transfers between devices, local(): lax.psum_scatter(gradient_rows(grad_gate_pre, grad_up_pre, hidden_k, keys...  666 us
    all_to_all x1, starting transfers between devices, local(): lax.all_to_all(first_block, 'head', split_axis=0, concat_axis=1, tiled=True)  91.3 us
    all_gather x1, blocking collectives, local(): lax.all_gather(w_down.astype(jnp.bfloat16), 'tok', axis=1, tiled=True)  76.5 us
    all_gather x1, blocking collectives, local(): lax.all_gather(down_new.astype(jnp.bfloat16), 'tok', axis=1, tiled=True)  73.4 us
    all_gather x1, blocking collectives, local(): lax.all_gather(w_up.astype(jnp.bfloat16), 'tok', axis=1, tiled=True)  73.1 us
    all_gather x1, blocking collectives, local(): lax.all_gather(gate_new.astype(jnp.bfloat16), 'tok', axis=1, tiled=True)  72.8 us
    all_gather x1, blocking collectives, local(): lax.all_gather(up_new.astype(jnp.bfloat16), 'tok', axis=1, tiled=True)  72.6 us
    all_gather x1, blocking collectives, local(): lax.all_gather(w_gate.astype(jnp.bfloat16), 'tok', axis=1, tiled=True)  71.9 us
  transfers between devices with their start and end apart: 8, of which 5 were waited for; matrix products, arithmetic and copies ran while one was open for 1% of the time, Pallas kernels for 0%

commit v1 on v0

--- a/solution.py
+++ b/solution.py
@@ -2,6 +2,18 @@
 import jax.numpy as jnp
 from jax import lax
 from jax.sharding import PartitionSpec as P
+
+
+def collect(x, axis, dim):
+    ways, here = (lax.axis_size(axis), lax.axis_index(axis))
+    grown, reach = (x, 1)
+    while reach < ways:
+        theirs = lax.ppermute(grown, axis, [(d, d ^ reach) for d in range(ways)])
+        mine_first = jnp.concatenate([grown, theirs], axis=dim)
+        theirs_first = jnp.concatenate([theirs, grown], axis=dim)
+        grown = jnp.where(here & reach == 0, mine_first, theirs_first)
+        reach = 2 * reach
+    return grown
 
 
 def apply_piece(query, gate_b, up_b, down_b):
@@ -57,7 +69,7 @@
     query_b = moved[4].reshape(tokens, heads_local, width)
     targets = (-(rates[:, :, None] * values.astype(jnp.float32))).astype(jnp.bfloat16)
     pieces = (
-        lax.all_gather(w_gate.astype(jnp.bfloat16), "tok", axis=1, tiled=True),
+        collect(w_gate.astype(jnp.bfloat16), "tok", 1),
         lax.all_gather(w_up.astype(jnp.bfloat16), "tok", axis=1, tiled=True),
         lax.all_gather(w_down.astype(jnp.bfloat16), "tok", axis=1, tiled=True),
     )

time: 1370 us -> 1330 us (0.971)
  blocking collectives: 440 us -> 368 us
  waiting for transfers between devices: 688 us -> 716 us
    all_gather x1 -> x0, blocking collectives: 71.9 us -> none  [local(): lax.all_gather(w_gate.astype(jnp.bfloat16), 'tok', axis=1, tiled=True)]
    all_to_all x1, starting transfers between devices: 55.9 us -> 8.22 us  [local(): lax.all_to_all(key_one, 'head', split_axis=1, concat_axis=0, tiled=True)]
    ppermute x0 -> x6, waiting for transfers between devices: none -> 28.3 us  [collect(): theirs = lax.ppermute(grown, axis, [(d, d ^ reach) for d in range(ways)])]
    all_to_all x1, starting transfers between devices: 30.4 us -> 56.7 us  [local(): lax.all_to_all(value_one, 'head', split_axis=1, concat_axis=0, tiled=True)]
    ppermute x0 -> x6, starting transfers between devices: none -> 22.3 us  [collect(): theirs = lax.ppermute(grown, axis, [(d, d ^ reach) for d in range(ways)])]
  transfers between devices with their start and end apart: 8 -> 14, of which waited for: 5 -> 10; matrix products, arithmetic and copies ran while one was open for 1% -> 1% of each run, Pallas kernels for 0% -> 0%
where the time goes in v1:
time: 1330 us
  waiting for transfers between devices  716 us (54%)
  blocking collectives  368 us (28%)
  starting transfers between devices  209 us (16%)
  between operations  14.9 us (1%)
    reduce_scatter x1, waiting for transfers between devices, local(): lax.psum_scatter(gradient_rows(grad_gate_pre, grad_up_pre, hidden_k, keys...  666 us
    all_to_all x1, starting transfers between devices, local(): lax.all_to_all(first_block, 'head', split_axis=0, concat_axis=1, tiled=True)  91.3 us
    all_gather x1, blocking collectives, local(): lax.all_gather(w_down.astype(jnp.bfloat16), 'tok', axis=1, tiled=True)  77.6 us
    all_gather x1, blocking collectives, local(): lax.all_gather(gate_new.astype(jnp.bfloat16), 'tok', axis=1, tiled=True)  73.1 us
    all_gather x1, blocking collectives, local(): lax.all_gather(up_new.astype(jnp.bfloat16), 'tok', axis=1, tiled=True)  72.8 us
    all_gather x1, blocking collectives, local(): lax.all_gather(down_new.astype(jnp.bfloat16), 'tok', axis=1, tiled=True)  72.7 us
    all_gather x1, blocking collectives, local(): lax.all_gather(w_up.astype(jnp.bfloat16), 'tok', axis=1, tiled=True)  72.2 us
    all_to_all x1, starting transfers between devices, local(): lax.all_to_all(value_one, 'head', split_axis=1, concat_axis=0, tiled=True)  56.7 us
  transfers between devices with their start and end apart: 14, of which 10 were waited for; matrix products, arithmetic and copies ran while one was open for 1% of the time, Pallas kernels for 0%

profile of v1, /device:TPU:1, one launch (start us, length us, event | category | flops | bytes accessed | tf_op | source)
XLA Modules:
  0.0 1330.6 jit_solution(11076202569131269778)
XLA Ops:
  7.2 0.7 convert_element_type.140
  7.9 4.0 collective-permute-start
  11.9 1.3 copy.56
  13.2 8.0 all-to-all-start.2
  21.2 0.7 convert_bitcast_fusion
  21.9 0.7 convert_element_type.143
  22.6 77.6 %all_gather.16 = bf16[1,512,512]{2,1,0:T(8,128)(2,1)S(1)} all-gather(bf16[1,8,512]{2,1,0:T(8,128)(2,1)S(1)} %convert_element_type.143), channel_id=1, replica_groups=mesh['head'=8,'tok'=64] {'tok'}, dimensions={1}, use_global_device_ids=true | all-gather | bytes 532480 | tf_op jit(solution)/shard_map/all_gather | solution.py:74
  100.2 0.7 convert_element_type.141
  100.9 72.2 %all_gather.15 = bf16[1,512,512]{2,1,0:T(8,128)(2,1)S(1)} all-gather(bf16[1,8,512]{2,1,0:T(8,128)(2,1)S(1)} %convert_element_type.141), channel_id=1, replica_groups=mesh['head'=8,'tok'=64] {'tok'}, dimensions={1}, use_global_device_ids=true | all-gather | bytes 532480 | tf_op jit(solution)/shard_map/all_gather | solution.py:73
  173.1 1.7 copy.82
  174.8 1.7 copy.81
  176.5 0.0 all-to-all-done.2
  176.5 56.7 %all-to-all-start.3 = ((bf16[32,8,512]{2,0,1:T(8,128)(2,1)}), bf16[32,8,512]{2,0,1:T(8,128)(2,1)S(1)}, u32[]{:S(2)}, u32[]{:S(2)}) async-start(bf16[32,8,512]{2,0,1:T(8,128)(2,1)} %bitcast.151), calls=%async_computation.3 | async-start | bytes 524288 | tf_op jit(solution)/shard_map/all_to_all | solution.py:60
  233.2 0.1 reshape.979
  233.3 0.0 collective-permute-done
  233.3 3.3 collective-permute-start.1
  236.6 2.7 collective-permute-done.1
  239.3 1.9 collective-permute-start.2
  241.2 2.7 collective-permute-done.2
  244.0 1.9 collective-permute-start.3
  245.9 4.4 collective-permute-done.3
  250.3 2.8 collective-permute-start.4
  253.2 0.0 all-to-all-done.3
  253.2 8.2 all-to-all-start.4
  261.5 0.0 reduce-scatter.2.cloned.1.call-start
  261.5 0.4 fusion.9
  261.9 6.3 all-to-all-done.4
  268.2 0.3 fusion.12
  268.6 0.7 collective-permute-done.4
  269.3 0.1 maximum_select_fusion.2
  269.4 8.4 collective-permute-start.5
  277.8 0.1 fusion.4
  277.9 0.1 maximum_select_fusion.1
  277.9 17.8 %collective-permute-done.5 = bf16[1,256,512]{2,1,0:T(8,128)(2,1)S(1)} collective-permute-done((bf16[1,256,512]{2,1,0:T(8,128)(2,1)S(1)}, bf16[1,256,512]{2,1,0:T(8,128)(2,1)S(1)}, u32[]{:S(2)}, u32[]{:S(2)}) %collective-permute-start.5) | collective-permute-done | bytes 262176 | tf_op jit(solution)/shard_map/ppermute | solution.py:11
  295.7 0.4 convolution_bitcast_fusion.5
  296.1 0.3 convolution_bitcast_fusion.1
  296.4 0.4 convolution_bitcast_fusion.2
  296.8 0.3 convolution_bitcast_fusion
  297.2 2.0 pad_maximum_fusion
  299.1 0.0 reduce-scatter.2.cloned.1.call-update
  299.1 0.9 copy-done
  300.1 0.7 copy.83
  300.8 14.2 %all-to-all-start = ((bf16[32,8,512]{2,0,1:T(8,128)(2,1)}), bf16[32,8,512]{2,0,1:T(8,128)(2,1)S(1)}, u32[]{:S(2)}, u32[]{:S(2)}) async-start(bf16[32,8,512]{2,0,1:T(8,128)(2,1)} %bitcast.152), calls=%async_computation | async-start | bytes 524288 | tf_op jit(solution)/shard_map/all_to_all | solution.py:58
  315.0 0.0 copy-done.1
  315.0 0.7 copy.80
  316.4 5.1 all-to-all-done
  321.5 4.4 all-to-all-start.5
  325.9 0.3 convolution_bitcast_fusion.6
  326.2 1.5 convolution_convert_fusion.1
  327.8 665.5 %reduce-scatter.2.cloned.1.call-done = f32[8,1,3,512]{3,0,2,1:T(8,128)} async-done(((f32[512,1,3,512]{3,0,2,1:T(8,128)}), f32[8,1,3,512]{3,0,2,1:T(8,128)}) %reduce-scatter.2.cloned.1.call-update) | async-done | bytes 49168 | tf_op jit(solution)/shard_map/reduce_scatter | solution.py:80
  993.3 0.9 multiply_reduce_fusion.1
  994.2 1.5 fusion.45
  995.7 72.8 %all_gather.19 = bf16[1,512,512]{2,1,0:T(8,128)(2,1)S(1)} all-gather(bf16[1,8,512]{2,1,0:T(8,128)(2,1)S(1)} %get-tuple-element.14), channel_id=1, replica_groups=mesh['head'=8,'tok'=64] {'tok'}, dimensions={1}, use_global_device_ids=true | all-gather | bytes 532480 | tf_op jit(solution)/shard_map/all_gather | solution.py:91
  1068.5 72.7 %all_gather.17 = bf16[1,512,512]{2,1,0:T(8,128)(2,1)S(1)} all-gather(bf16[1,8,512]{2,1,0:T(8,128)(2,1)S(1)} %get-tuple-element.16), channel_id=1, replica_groups=mesh['head'=8,'tok'=64] {'tok'}, dimensions={1}, use_global_device_ids=true | all-gather | bytes 532480 | tf_op jit(solution)/shard_map/all_gather | solution.py:92
  1141.2 73.1 %all_gather.18 = bf16[1,512,512]{2,1,0:T(8,128)(2,1)S(1)} all-gather(bf16[1,8,512]{2,1,0:T(8,128)(2,1)S(1)} %get-tuple-element.8), channel_id=1, replica_groups=mesh['head'=8,'tok'=64] {'tok'}, dimensions={1}, use_global_device_ids=true | all-gather | bytes 532480 | tf_op jit(solution)/shard_map/all_gather | solution.py:90
  1214.3 0.0 all-to-all-done.5
  1214.3 91.3 %all-to-all-start.1 = ((bf16[8,32,512]{2,1,0:T(8,128)(2,1)}), bf16[8,32,512]{2,1,0:T(8,128)(2,1)S(1)}, u32[]{:S(2)}, u32[]{:S(2)}) async-start(bf16[8,32,512]{2,1,0:T(8,128)(2,1)} %bitcast.20), calls=%async_computation.1 | async-start | bytes 524288 | tf_op jit(solution)/shard_map/all_to_all | solution.py:97
  1305.6 0.3 convolution_bitcast_fusion.4
  1305.9 1.5 convolution_convert_fusion
  1307.5 4.7 all-to-all-done.1
  1312.1 4.4 all-to-all-start.6
  1316.5 0.7 copy.74
  1317.2 5.8 all-to-all-done.6
  1323.0 0.7 copy.75
  (20 shorter events, 0.2 us)
Async XLA Ops:
  7.9 225.4 %collective-permute-start = (bf16[1,8,512]{2,1,0:T(8,128)(2,1)S(1)}, bf16[1,8,512]{2,1,0:T(8,128)(2,1)S(1)}, u32[]{:S(2)}, u32[]{:S(2)}) collective-permute-start(bf16[1,8,512]{2,1,0:T(8,128)(2,1)S(1)} %convert_element_type.140), channel_id=1, source_target_pairs={{0,1},{1,0},{2,3},{3,2},{4,5},{5,4},{6,7},{7,6},{8,9},{9,8},{10,11... | collective-permute-start | bytes 24584 | tf_op jit(solution)/shard_map/ppermute | solution.py:11
  13.2 163.3 %all-to-all-start.2 = ((bf16[32,8,1]{0,2,1:T(2,128)(2,1)}), bf16[32,8,1]{0,2,1:T(2,128)(2,1)S(1)}, u32[]{:S(2)}, u32[]{:S(2)}) async-start(bf16[32,8,1]{0,2,1:T(2,128)(2,1)} %copy.56), calls=%async_computation.2 | async-start | bytes 8192 | tf_op jit(solution)/shard_map/all_to_all | solution.py:61
  176.5 76.7 %all-to-all-start.3 = ((bf16[32,8,512]{2,0,1:T(8,128)(2,1)}), bf16[32,8,512]{2,0,1:T(8,128)(2,1)S(1)}, u32[]{:S(2)}, u32[]{:S(2)}) async-start(bf16[32,8,512]{2,0,1:T(8,128)(2,1)} %bitcast.151), calls=%async_computation.3 | async-start | bytes 524288 | tf_op jit(solution)/shard_map/all_to_all | solution.py:60
  233.3 6.0 collective-permute-start.1
  239.3 4.7 collective-permute-start.2
  244.0 6.3 collective-permute-start.3
  250.3 19.0 %collective-permute-start.4 = (bf16[1,128,512]{2,1,0:T(8,128)(2,1)S(1)}, bf16[1,128,512]{2,1,0:T(8,128)(2,1)S(1)}, u32[]{:S(2)}, u32[]{:S(2)}) collective-permute-start(bf16[1,128,512]{2,1,0:T(8,128)(2,1)S(1)} %maximum_select_fusion.4), channel_id=1, source_target_pairs={{0,16},{1,17},{2,18},{3,19},{4,20},{5,21},{6,22},{7,23},{8,24},{9,... | collective-permute-start | bytes 393224 | tf_op jit(solution)/shard_map/ppermute | solution.py:11
  253.2 15.0 %all-to-all-start.4 = ((bf16[32,8,512]{2,0,1:T(8,128)(2,1)}), bf16[32,8,512]{2,0,1:T(8,128)(2,1)S(1)}, u32[]{:S(2)}, u32[]{:S(2)}) async-start(bf16[32,8,512]{2,0,1:T(8,128)(2,1)} %bitcast.150), calls=%async_computation.4 | async-start | bytes 524288 | tf_op jit(solution)/shard_map/all_to_all | solution.py:59
  261.5 731.8 %reduce-scatter.2.cloned.1.call-start = ((), (), s32[]{:S(2)}) async-start(), calls=%async_computation.8 | async-start | bytes 3194880 | tf_op jit(solution)/shard_map/reduce_scatter | solution.py:80
  269.4 26.3 %collective-permute-start.5 = (bf16[1,256,512]{2,1,0:T(8,128)(2,1)S(1)}, bf16[1,256,512]{2,1,0:T(8,128)(2,1)S(1)}, u32[]{:S(2)}, u32[]{:S(2)}) collective-permute-start(bf16[1,256,512]{2,1,0:T(8,128)(2,1)S(1)} %maximum_select_fusion.2), channel_id=1, source_target_pairs={{0,32},{1,33},{2,34},{3,35},{4,36},{5,37},{6,38},{7,39},{8,40},{9,... | collective-permute-start | bytes 786440 | tf_op jit(solution)/shard_map/ppermute | solution.py:11
  299.1 0.9 copy-start
  299.1 15.9 %copy-start.1 = (bf16[32,4096]{1,0:T(8,128)(2,1)S(1)}, bf16[32,4096]{1,0:T(8,128)(2,1)}, u32[]{:S(2)}) copy-start(bf16[32,4096]{1,0:T(8,128)(2,1)} %param.13) | copy-start | bytes 786436
  300.8 20.7 %all-to-all-start = ((bf16[32,8,512]{2,0,1:T(8,128)(2,1)}), bf16[32,8,512]{2,0,1:T(8,128)(2,1)S(1)}, u32[]{:S(2)}, u32[]{:S(2)}) async-start(bf16[32,8,512]{2,0,1:T(8,128)(2,1)} %bitcast.152), calls=%async_computation | async-start | bytes 524288 | tf_op jit(solution)/shard_map/all_to_all | solution.py:58
  321.5 892.8 %all-to-all-start.5 = ((bf16[32,8,512]{2,0,1:T(8,128)(2,1)}), bf16[32,8,512]{2,0,1:T(8,128)(2,1)S(1)}, u32[]{:S(2)}, u32[]{:S(2)}) async-start(bf16[32,8,512]{2,0,1:T(8,128)(2,1)} %bitcast.149), calls=%async_computation.6 | async-start | bytes 524288 | tf_op jit(solution)/shard_map/all_to_all | solution.py:62
  325.9 668.3 %copy-start.2 = (f32[1,8,512]{2,1,0:T(8,128)S(1)}, f32[1,8,512]{2,1,0:T(8,128)}, u32[]{:S(2)}) copy-start(f32[1,8,512]{2,1,0:T(8,128)} %param.14) | copy-start | bytes 49156
  325.9 668.3 %copy-start.3 = (f32[1,8,512]{2,1,0:T(8,128)S(1)}, f32[1,8,512]{2,1,0:T(8,128)}, u32[]{:S(2)}) copy-start(f32[1,8,512]{2,1,0:T(8,128)} %param.16) | copy-start | bytes 49156
  325.9 668.4 %copy-start.4 = (f32[1,8,512]{2,1,0:T(8,128)S(1)}, f32[1,8,512]{2,1,0:T(8,128)}, u32[]{:S(2)}) copy-start(f32[1,8,512]{2,1,0:T(8,128)} %param.15) | copy-start | bytes 49156
  1214.3 97.8 %all-to-all-start.1 = ((bf16[8,32,512]{2,1,0:T(8,128)(2,1)}), bf16[8,32,512]{2,1,0:T(8,128)(2,1)S(1)}, u32[]{:S(2)}, u32[]{:S(2)}) async-start(bf16[8,32,512]{2,1,0:T(8,128)(2,1)} %bitcast.20), calls=%async_computation.1 | async-start | bytes 524288 | tf_op jit(solution)/shard_map/all_to_all | solution.py:97
  1312.1 10.9 all-to-all-start.6
Sparse Core Ops, SparseCore 0:
  299.3 693.9 reduce-scatter.1
